TPU v7x, 32 devices: a whole 2x2x4 slice. The times are simulated.
32 devices in a mesh: dp: 4 (over z), mp: 8 (over y, x, core).
Axes of the slice: x: 2, y: 2, z: 4, core: 2. Of those that a mesh axis runs over, the one named last changes fastest.
Arguments:
- tokens_in: bfloat16 [2048, 3072], P(('dp', 'mp')), may hold values from -6 to 6
- out_grad: bfloat16 [2048, 3072], P(('dp', 'mp')), may hold values from -0.29882812 to 0.29882812
- w_up: bfloat16 [12288, 3072], P('mp'), may hold values from -0.109375 to 0.109375
- w_down: bfloat16 [12288, 3072], P('mp'), may hold values from -0.0546875 to 0.0546875
- mask_up: int32 [96, 24], P('mp'), may hold values 0 or 1
- mask_down: int32 [96, 24], P('mp'), may hold values 0 or 1
- order_up: int32 [48], replicated, may hold values from 0 to 47, each once
- order_down: int32 [48], replicated, may hold values from 0 to 47, each once
- moment_one: float32 [2, 8, 48, 32, 3072], P(None, 'mp', 'dp'), may hold values from -1.8 to 1.8
- moment_two: float32 [2, 8, 48, 32, 3072], P(None, 'mp', 'dp'), may hold values from 0.03 to 1
Outputs:
- input_grad: bfloat16 [2048, 3072], P(('dp', 'mp'))
- update_step: bfloat16 [2, 12288, 3072], P(None, 'mp')
Inputs may be any that keep to these rules, and one draw needn't show every extreme that they name: `order_up`: each value of 0 to 47 appears once. `order_down`: each value of 0 to 47 appears once.
All inputs are finite; a program needn't handle non-finite values. No bound on the sum of `mask_up` or of `mask_down` on one device may be relied on, other than what follows from the above.
Results may differ from a plain program's by a relative error of at most 0.014.
Values may be sent and summed in bfloat16 or wider, within the bound.
A program may use at most 192 MiB of HBM per device.

v0:
```python
import jax
import jax.numpy as jnp
from jax import lax
from jax.sharding import PartitionSpec as P

bias_first = 1.0 - 0.9**10
bias_second = 1.0 - 0.95**10


def expand_mask(blocks):
    block_rows, block_cols = blocks.shape
    wide = jnp.broadcast_to(
        blocks.astype(jnp.bfloat16)[:, None, :, None], (block_rows, 128, block_cols, 128)
    )
    return wide.reshape(block_rows * 128, block_cols * 128)


def adam_step(summed, moment_a, moment_b, weight_rows, mask_rows):
    first_new = 0.9 * moment_a + 0.1 * summed
    second_new = 0.95 * moment_b + 0.05 * summed * summed
    update = first_new / bias_first / (jnp.sqrt(second_new / bias_second) + 1e-08)
    return (mask_rows * (update + 0.1 * weight_rows)).astype(jnp.bfloat16)


def slot_places(order_table, owners, owned):
    return order_table % owners * owned + order_table // owners


def shards(
    tokens_in,
    out_grad,
    w_up,
    w_down,
    mask_up,
    mask_down,
    order_up,
    order_down,
    moment_one,
    moment_two,
):
    owners = lax.axis_size("dp")
    hidden_local, width = w_up.shape
    buckets = order_up.shape[0]
    owned = buckets // owners
    bucket_rows = hidden_local // buckets
    keep_up = expand_mask(mask_up)
    keep_down = expand_mask(mask_down)
    up_live = w_up * keep_up
    down_live = w_down * keep_down
    place_up = slot_places(order_up, owners, owned)
    place_down = slot_places(order_down, owners, owned)
    sorter_up = jnp.argsort(place_up)
    sorter_down = jnp.argsort(place_down)

    def owner_order(matrix, sorter):
        return matrix.reshape(buckets, bucket_rows, width)[sorter]

    feat_rows, grad_rows = (
        lax.all_gather(tokens_in, "mp", axis=0, tiled=True),
        lax.all_gather(out_grad, "mp", axis=0, tiled=True),
    )
    hidden_pre = jnp.einsum("td,fd->tf", feat_rows, up_live, preferred_element_type=jnp.float32)
    activation, gelu_back = jax.vjp(jax.nn.gelu, hidden_pre)
    act_low = activation.astype(jnp.bfloat16)
    grad_down = (
        jnp.einsum("tf,td->fd", act_low, grad_rows, preferred_element_type=jnp.float32) * keep_down
    ).astype(jnp.bfloat16)
    down_sorted = owner_order(grad_down, sorter_down)
    act_grad = jnp.einsum("td,fd->tf", grad_rows, down_live, preferred_element_type=jnp.float32)
    hidden_grad = gelu_back(act_grad)[0].astype(jnp.bfloat16)
    grad_up = (
        jnp.einsum("tf,td->fd", hidden_grad, feat_rows, preferred_element_type=jnp.float32)
        * keep_up
    ).astype(jnp.bfloat16)
    up_sorted = owner_order(grad_up, sorter_up)
    up_summed, down_summed = (
        lax.psum_scatter(up_sorted, "dp", scatter_dimension=0, tiled=True).astype(jnp.float32),
        lax.psum_scatter(down_sorted, "dp", scatter_dimension=0, tiled=True).astype(jnp.float32),
    )
    partial_term = jnp.dot(hidden_grad, up_live, preferred_element_type=jnp.float32)
    input_grad = lax.psum_scatter(
        lax.optimization_barrier(partial_term.astype(jnp.bfloat16))
        .astype(jnp.float32)
        .astype(jnp.bfloat16),
        "mp",
        scatter_dimension=0,
        tiled=True,
    )
    owner_index = lax.axis_index("dp")

    def owned_rows(matrix, sorter):
        chosen = lax.dynamic_slice_in_dim(sorter, owner_index * owned, owned, 0)
        return matrix.reshape(buckets, bucket_rows, width)[chosen].astype(jnp.float32)

    step_up = adam_step(
        up_summed,
        moment_one[0, 0],
        moment_two[0, 0],
        owned_rows(w_up, sorter_up),
        owned_rows(keep_up, sorter_up),
    )
    step_down = adam_step(
        down_summed,
        moment_one[1, 0],
        moment_two[1, 0],
        owned_rows(w_down, sorter_down),
        owned_rows(keep_down, sorter_down),
    )
    stacked = jnp.stack([step_up, step_down])
    all_steps = lax.all_gather(stacked, "dp", axis=1, tiled=True)
    update_up = all_steps[0][place_up].reshape(hidden_local, width)
    update_down = all_steps[1][place_down].reshape(hidden_local, width)
    return (input_grad, jnp.stack([update_up, update_down]))


def solution(mesh):
    placed = (
        P(("dp", "mp"), None),
        P(("dp", "mp"), None),
        P("mp", None),
        P("mp", None),
        P("mp", None),
        P("mp", None),
        P(),
        P(),
        P(None, "mp", "dp", None, None),
        P(None, "mp", "dp", None, None),
    )
    return jax.shard_map(
        shards,
        mesh=mesh,
        in_specs=placed,
        out_specs=(P(("dp", "mp"), None), P(None, "mp", None)),
        check_vma=False,
    )
```

profile of v0, /device:TPU:0, one launch (start us, length us, event | category | flops | bytes accessed | tf_op | source)
XLA Modules:
  0.0 839.3 jit_solution(18346373174913649701)
XLA Ops:
  8.7 0.7 convert_element_type.54
  10.8 2.0 sort.31
  12.8 32.1 %all-gather.6.cloned.1.call-done = bf16[512,3072]{1,0:T(8,128)(2,1)} async-done(((bf16[64,3072]{1,0:T(8,128)(2,1)}), bf16[512,3072]{1,0:T(8,128)(2,1)}) %all-gather.6.cloned.1.call-update) | async-done | bytes 3145744 | tf_op jit(solution)/shard_map/all_gather | solution.py:59
  45.0 1.3 broadcast_in_dim.45
  46.3 4.8 copy-done
  51.0 1.0 copy-done.1
  52.0 8.8 %convolution_bitcast_fusion = f32[512,1536]{0,1:T(8,128)} fusion(bf16[512,3072]{1,0:T(8,128)(2,1)} %all-gather.6.cloned.1.call-done, bf16[1536,3072]{1,0:T(8,128)(2,1)S(1)} %copy-done.1, bf16[192,8,24,128]{3,2,1,0:T(8,128)(2,1)S(1)} %bitcast.79), kind=kOutput, calls=%fused_computation.46 | convolution fusion | flops 4836556800 | bytes 25165824 | tf_op jit(solution)/shard_map/td,fd->tf/dot_general | solution.py:62
  60.9 18.3 %all-gather.4.cloned.1.call-done = bf16[512,3072]{1,0:T(8,128)(2,1)} async-done(((bf16[64,3072]{1,0:T(8,128)(2,1)}), bf16[512,3072]{1,0:T(8,128)(2,1)}) %all-gather.4.cloned.1.call-update) | async-done | bytes 3145744 | tf_op jit(solution)/shard_map/all_gather | solution.py:60
  79.2 5.4 broadcast_in_dim.44
  84.6 12.4 %fusion.29 = bf16[512,1536]{0,1:T(8,128)(2,1)} fusion(f32[512,1536]{0,1:T(8,128)} %convolution_bitcast_fusion, bf16[512,3072]{1,0:T(8,128)(2,1)S(1)} %copy-done.2, bf16[1536,3072]{1,0:T(8,128)(2,1)} %param.13, bf16[192,8,24,128]{3,2,1,0:T(8,128)(2,1)} %bitcast.84), kind=kOutput, calls=%fused_computation.53 | convolution fusion | flops 4852285440 | bytes 26738688 | tf_op jit(solution)/shard_map/td,fd->tf/dot_general | solution.py:69
  97.1 9.7 %multiply_convert_fusion.1 = bf16[1536,3072]{1,0:T(8,128)(2,1)} fusion(bf16[512,1536]{0,1:T(8,128)(2,1)} %fusion.29, bf16[512,3072]{1,0:T(8,128)(2,1)S(1)} %copy-done.3, bf16[192,8,24,128]{3,2,1,0:T(8,128)(2,1)S(1)} %bitcast.83), kind=kOutput, calls=%fused_computation.10 | convolution fusion | flops 4845993984 | bytes 23592960 | tf_op jit(solution)/shard_map/tf,td->fd/dot_general | solution.py:72
  106.8 10.0 %gather_fusion.1 = bf16[48,32,3072]{2,1,0:T(8,128)(2,1)} fusion(bf16[48,32,3072]{2,1,0:T(8,128)(2,1)} %bitcast.87, s32[1024]{0:T(1024)S(1)} %pad_clamp_fusion.4), kind=kCustom, calls=%fused_computation.1 | custom fusion | bytes 18874560 | tf_op jit(solution)/shard_map/gather | solution.py:56
  117.4 2.0 sort.32
  119.5 12.4 %multiply_convert_fusion = bf16[1536,3072]{1,0:T(8,128)(2,1)} fusion(bf16[512,3072]{1,0:T(8,128)(2,1)} %all-gather.4.cloned.1.call-done, bf16[192,8,24,128]{3,2,1,0:T(8,128)(2,1)} %bitcast.85, f32[512,1536]{0,1:T(8,128)} %convolution_bitcast_fusion), kind=kOutput, calls=%fused_computation.9 | convolution fusion | flops 4853071872 | bytes 25165824 | tf_op jit(solution)/shard_map/tf,td->fd/dot_general | solution.py:66
  131.9 10.2 %gather_fusion.4 = bf16[48,32,3072]{2,1,0:T(8,128)(2,1)} fusion(bf16[48,32,3072]{2,1,0:T(8,128)(2,1)} %bitcast.86, s32[1024]{0:T(1024)S(1)} %pad_clamp_fusion.2), kind=kCustom, calls=%fused_computation.4 | custom fusion | bytes 18874560 | tf_op jit(solution)/shard_map/gather | solution.py:56
  142.7 4.5 gather_fusion.2
  147.2 5.0 broadcast_in_dim.48
  152.1 5.9 gather_fusion
  158.2 5.8 gather_fusion.5
  164.0 5.0 broadcast_in_dim.53
  169.0 5.8 gather_fusion.3
  174.8 103.4 %reduce-scatter.6.cloned.1.call-done = bf16[12,32,3072]{2,1,0:T(8,128)(2,1)} async-done(((bf16[48,32,3072]{2,1,0:T(8,128)(2,1)}), bf16[12,32,3072]{2,1,0:T(8,128)(2,1)}) %reduce-scatter.6.cloned.1.call-update) | async-done | bytes 2359312 | tf_op jit(solution)/shard_map/reduce_scatter | solution.py:77
  278.2 164.4 %reduce-scatter.8.cloned.1.call-done = bf16[12,32,3072]{2,1,0:T(8,128)(2,1)} async-done(((bf16[48,32,3072]{2,1,0:T(8,128)(2,1)}), bf16[12,32,3072]{2,1,0:T(8,128)(2,1)}) %reduce-scatter.8.cloned.1.call-update) | async-done | bytes 2359312 | tf_op jit(solution)/shard_map/reduce_scatter | solution.py:78
  442.6 13.2 %fusion.30 = (bf16[1,12,32,3072]{3,2,1,0:T(8,128)(2,1)S(1)}, bf16[1,12,32,3072]{3,2,1,0:T(8,128)(2,1)S(1)}) fusion(bf16[12,32,3072]{2,1,0:T(8,128)(2,1)S(1)} %gather_fusion.2, f32[2,1,12,32,3072]{4,3,2,1,0:T(8,128)} %param.19, bf16[12,32,3072]{2,1,0:T(8,128)(2,1)} %reduce-scatter.6.cloned.1.call-done, f32[2,1,12,32,3072]{4,3,2,1,0:T(8,128)} %param.18, ...), kind=kLoop, calls=%fused_computation.55 | loop fusion | flops 42467328 | bytes 37748736 | tf_op jit(solution)/shard_map/stack | solution.py:109
  455.8 2.6 pad_maximum_fusion.1
  458.5 1.3 copy-done.5
  459.8 13.4 %convolution_convert_fusion = bf16[512,3072]{1,0:T(8,128)(2,1)} fusion(bf16[512,1536]{0,1:T(8,128)(2,1)S(1)} %copy-done.5, bf16[1536,3072]{1,0:T(8,128)(2,1)} %param.12, bf16[192,8,24,128]{3,2,1,0:T(8,128)(2,1)} %bitcast.80), kind=kOutput, calls=%fused_computation.44 | convolution fusion | flops 4838129664 | bytes 23592960 | tf_op jit(solution)/shard_map/dot_general | solution.py:80
  473.3 307.4 %all-gather.8.cloned.1.call-done = bf16[2,48,32,3072]{3,2,1,0:T(8,128)(2,1)} async-done(((bf16[2,12,32,3072]{3,2,1,0:T(8,128)(2,1)}), bf16[2,48,32,3072]{3,2,1,0:T(8,128)(2,1)}) %all-gather.8.cloned.1.call-update) | async-done | bytes 18874384 | tf_op jit(solution)/shard_map/all_gather | solution.py:110
  780.7 14.8 %slice_bitcast_fusion.1 = (bf16[48,32,3072]{2,1,0:T(8,128)(2,1)}, bf16[48,32,3072]{2,1,0:T(8,128)(2,1)}) fusion(bf16[2,48,32,3072]{3,2,1,0:T(8,128)(2,1)} %all-gather.8.cloned.1.call-done), kind=kLoop, calls=%fused_computation.15 | loop fusion | bytes 37748736 | tf_op jit(solution)/shard_map/squeeze | solution.py:111
  795.5 10.3 %gather_fusion.7 = bf16[48,32,3072]{2,1,0:T(8,128)(2,1)} fusion(bf16[48,32,3072]{2,1,0:T(8,128)(2,1)} %get-tuple-element.11, s32[1024]{0:T(1024)S(1)} %pad_clamp_fusion), kind=kCustom, calls=%fused_computation.7 | custom fusion | bytes 18874560 | tf_op jit(solution)/shard_map/gather | solution.py:112
  805.8 10.2 %gather_fusion.6 = bf16[48,32,3072]{2,1,0:T(8,128)(2,1)} fusion(bf16[48,32,3072]{2,1,0:T(8,128)(2,1)} %get-tuple-element.10, s32[1024]{0:T(1024)S(1)} %pad_clamp_fusion.1), kind=kCustom, calls=%fused_computation.6 | custom fusion | bytes 18874560 | tf_op jit(solution)/shard_map/gather | solution.py:111
  816.0 16.5 %pad_maximum_fusion = bf16[2,1536,3072]{2,1,0:T(8,128)(2,1)} fusion(bf16[1,1536,3072]{2,1,0:T(8,128)(2,1)} %bitcast.77, bf16[1,1536,3072]{2,1,0:T(8,128)(2,1)} %bitcast.78), kind=kLoop, calls=%fused_computation.8 | loop fusion | flops 9437184 | bytes 37748736 | tf_op jit(solution)/shard_map/stack | solution.py:113
  (47 shorter events, 4.3 us)
Async XLA Ops:
  7.2 37.8 %all-gather.6.cloned.1.call-start = ((), (), s32[]{:S(2)}) async-start(), calls=%async_computation.4 | async-start | bytes 3538944 | tf_op jit(solution)/shard_map/all_gather | solution.py:59
  7.9 71.3 %all-gather.4.cloned.1.call-start = ((), (), s32[]{:S(2)}) async-start(), calls=%async_computation.3 | async-start | bytes 3538944 | tf_op jit(solution)/shard_map/all_gather | solution.py:60
  8.6 269.6 %reduce-scatter.6.cloned.1.call-start = ((), (), s32[]{:S(2)}) async-start(), calls=%async_computation.6 | async-start | bytes 11796480 | tf_op jit(solution)/shard_map/reduce_scatter | solution.py:77
  45.0 7.1 copy-start.1
  46.2 4.8 copy-start
  79.2 5.4 copy-start.2
  79.2 17.8 %slice-start = ((s8[9437184]{0:T(1024)(128)(4,1)}), s8[4194304]{0:T(1024)(128)(4,1)S(1)}, s32[]{:S(2)}) async-start(s8[9437184]{0:T(1024)(128)(4,1)} %bitcast.81), calls=%async_computation.9 | async-start | bytes 8388608
  84.6 12.4 %slice-start.1 = ((s8[9437184]{0:T(1024)(128)(4,1)}), s8[4194304]{0:T(1024)(128)(4,1)S(1)}, s32[]{:S(2)}) async-start(s8[9437184]{0:T(1024)(128)(4,1)} %bitcast.81), calls=%async_computation.10 | async-start | bytes 8388608
  84.6 12.4 %slice-start.2 = ((s8[9437184]{0:T(1024)(128)(4,1)}), s8[1048576]{0:T(1024)(128)(4,1)S(1)}, s32[]{:S(2)}) async-start(s8[9437184]{0:T(1024)(128)(4,1)} %bitcast.81), calls=%async_computation.11 | async-start | bytes 2097152
  84.6 12.4 %copy-start.3 = (bf16[512,3072]{1,0:T(8,128)(2,1)S(1)}, bf16[512,3072]{1,0:T(8,128)(2,1)}, u32[]{:S(2)}) copy-start(bf16[512,3072]{1,0:T(8,128)(2,1)} %all-gather.6.cloned.1.call-done) | copy-start | bytes 9437188
  116.8 0.7 copy-start.4
  116.8 325.8 %reduce-scatter.8.cloned.1.call-start = ((), (), s32[]{:S(2)}) async-start(), calls=%async_computation.7 | async-start | bytes 11796480 | tf_op jit(solution)/shard_map/reduce_scatter | solution.py:78
  142.2 638.5 %all-gather.8.cloned.1.call-start = ((), (), s32[]{:S(2)}) async-start(), calls=%async_computation.8 | async-start | bytes 23592960 | tf_op jit(solution)/shard_map/all_gather | solution.py:110
  458.4 1.4 copy-start.5
  458.4 374.1 %reduce-scatter.4.cloned.1.call-start = ((), (), s32[]{:S(2)}) async-start(), calls=%async_computation.5 | async-start | bytes 3538944 | tf_op jit(solution)/shard_map/reduce_scatter | solution.py:81
Sparse Core Ops, SparseCore 0:
  9.9 35.0 all-gather.5
  46.8 32.3 all-gather.3
  116.9 161.2 reduce-scatter.5
  280.4 162.1 reduce-scatter.7
  458.6 322.0 all-gather.7
  784.5 44.3 reduce-scatter.3
where the time goes:
time: 840 us; the launch traced here: 839 us
  waiting for transfers between devices  627 us (75%)
  local copies, waits for them, and re-layouts  102 us (12%)
  matrix products  56.8 us (7%)
  other arithmetic  38.6 us (5%)
  between operations  14.3 us (2%)
    all_gather x1, waiting for transfers between devices, shards(): all_steps = lax.all_gather(stacked, 'dp', axis=1, tiled=True)  307 us
    reduce_scatter x1, waiting for transfers between devices, shards(): lax.psum_scatter(down_sorted, 'dp', scatter_dimension=0, tiled=True)  164 us
    reduce_scatter x1, waiting for transfers between devices, shards(): lax.psum_scatter(up_sorted, 'dp', scatter_dimension=0, tiled=True)  103 us
    all_gather x1, waiting for transfers between devices, shards(): lax.all_gather(tokens_in, 'mp', axis=0, tiled=True)  32.1 us
    gather x4, local copies, waits for them, and re-layouts, owned_rows(): matrix.reshape(buckets, bucket_rows, width)[chosen].astype(jnp.float32)  22 us
    gather x2, local copies, waits for them, and re-layouts, owner_order(): return matrix.reshape(buckets, bucket_rows, width)[sorter]  20.2 us
    all_gather x1, waiting for transfers between devices, shards(): lax.all_gather(out_grad, 'mp', axis=0, tiled=True)  18.3 us
    broadcast_in_dim x6, local copies, waits for them, and re-layouts, expand_mask(): jnp.broadcast_to(blocks.astype(jnp.bfloat16)[:, None, :, None], (block_ro...  16.8 us
  transfers between devices with their start and end apart: 6, of which 5 were waited for; matrix products, arithmetic and copies ran while one was open for 16% of the time, Pallas kernels for 0%

commit v1 on v0

v1 whole, which is shorter than its diff:
```python
import functools

import jax
import jax.numpy as jnp
from jax import lax
from jax.experimental import pallas as pl
from jax.experimental.pallas import tpu as pltpu
from jax.sharding import PartitionSpec as P

MESH = pl.DeviceIdType.MESH
bias_first = 1.0 - 0.9**10
bias_second = 1.0 - 0.95**10


def gather_kernel(
    n_dp, n_mp, x_ref, g_ref, x_all, g_all, z_send, z_recv, r_send, r_recv, c_send, c_recv, l_sem
):
    d, m = lax.axis_index("dp"), lax.axis_index("mp")
    n = n_mp // 2
    q, core = m // 2, m % 2
    y, x = q // 2, q % 2
    spot = y + x * (n - 1 - 2 * y)

    def chip_at(p):
        far = p // (n // 2)
        return 2 * (p + far * (n - 1 - 2 * p)) + far

    sibling = q * 2 + 1 - core
    ahead = chip_at((spot + 1) % n) * 2 + core
    behind = chip_at((spot + n - 1) % n) * 2 + core
    offsets = [0]
    for k in range(1, n_dp):
        step = (k + 1) // 2
        offsets.append(step if k % 2 == 1 else n_dp - step)

    barrier = pltpu.get_barrier_semaphore()
    partners = [((d + k) % n_dp, m) for k in range(1, n_dp)]
    partners += [(d, ahead), (d, behind), (d, sibling)]
    for partner in partners:
        pl.semaphore_signal(barrier, inc=1, device_id=partner, device_id_type=MESH)
    pl.semaphore_wait(barrier, len(partners))

    own = (x_ref, g_ref)
    full = (x_all, g_all)
    turn = (1, n - 1)
    onward = (ahead, behind)

    def slot(arr, e, s, c):
        p = (spot + n - turn[arr] * s % n) % n
        return ((d + n_dp - offsets[e]) % n_dp) * n_mp + chip_at(p) * 2 + c

    def copy(src, dst, send, recv, device):
        return pltpu.make_async_remote_copy(
            src_ref=src,
            dst_ref=dst,
            send_sem=send,
            recv_sem=recv,
            device_id=device,
            device_id_type=MESH,
        )

    sends, locals_ = [], []

    def pass_on(arr, e, s):
        place = full[arr].at[slot(arr, e, s, core)]
        source = own[arr] if e == 0 and s == 0 else place
        if s < n - 1:
            sent = copy(
                source, place, r_send.at[arr, e, s], r_recv.at[arr, e, s + 1], (d, onward[arr])
            )
            sent.start()
            sends.append(sent)
        sent = copy(source, place, c_send.at[arr, e, s], c_recv.at[arr, e, s], (d, sibling))
        sent.start()
        sends.append(sent)

    for arr in range(2):
        pass_on(arr, 0, 0)
    for e in range(1, n_dp):
        for arr in range(2):
            sent = copy(
                own[arr],
                full[arr].at[d * n_mp + m],
                z_send.at[arr, e],
                z_recv.at[arr, e],
                ((d + offsets[e]) % n_dp, m),
            )
            sent.start()
            sends.append(sent)
    for arr in range(2):
        kept = pltpu.make_async_copy(own[arr], full[arr].at[d * n_mp + m], l_sem.at[arr])
        kept.start()
        locals_.append(kept)
    for wave in range(1, n_dp + n - 1):
        for e in range(n_dp):
            s = wave - e
            if s < 0 or s >= n:
                continue
            for arr in range(2):
                place = full[arr].at[slot(arr, e, s, core)]
                if s == 0:
                    copy(place, place, z_send.at[arr, e], z_recv.at[arr, e], (d, sibling)).wait_recv()
                else:
                    copy(
                        place, place, r_send.at[arr, e, s], r_recv.at[arr, e, s], (d, sibling)
                    ).wait_recv()
                pass_on(arr, e, s)
    for e in range(n_dp):
        for s in range(n):
            for arr in range(2):
                place = full[arr].at[slot(arr, e, s, 1 - core)]
                copy(
                    place, place, c_send.at[arr, e, s], c_recv.at[arr, e, s], (d, sibling)
                ).wait_recv()
    for sent in sends:
        sent.wait_send()
    for kept in locals_:
        kept.wait()


def gather_all(x, g, n_dp, n_mp):
    rows, width = x.shape
    n = n_mp // 2
    shape = jax.ShapeDtypeStruct((n_dp * n_mp, rows, width), x.dtype)
    any_spec = pl.BlockSpec(memory_space=pl.ANY)
    out = pl.pallas_call(
        functools.partial(gather_kernel, n_dp, n_mp),
        out_shape=(shape, shape),
        in_specs=[any_spec, any_spec],
        out_specs=(any_spec, any_spec),
        scratch_shapes=[
            pltpu.SemaphoreType.DMA((2, n_dp)),
            pltpu.SemaphoreType.DMA((2, n_dp)),
            pltpu.SemaphoreType.DMA((2, n_dp, n)),
            pltpu.SemaphoreType.DMA((2, n_dp, n)),
            pltpu.SemaphoreType.DMA((2, n_dp, n)),
            pltpu.SemaphoreType.DMA((2, n_dp, n)),
            pltpu.SemaphoreType.DMA((2,)),
        ],
        compiler_params=pltpu.CompilerParams(collective_id=0, has_side_effects=True),
        name="gather_tokens",
    )(x, g)
    return tuple(a.reshape(n_dp * n_mp * rows, width) for a in out)


def step_kernel(cols, owned, pos_ref, gu, gd, wu, wd, ma, mb, out):
    s, i = pl.program_id(0), pl.program_id(1)
    base = (s * owned + i) * cols

    def run(g_ref, w_ref):
        for c in range(cols):
            at = slice(c * 128, (c + 1) * 128)
            g = g_ref[0, :, at]
            first_new = 0.9 * ma[0, 0, 0, :, at] + 0.1 * g
            second_new = 0.95 * mb[0, 0, 0, :, at] + 0.05 * g * g
            update = first_new / bias_first / (jnp.sqrt(second_new / bias_second) + 1e-08)
            step = update + 0.1 * w_ref[0, :, at].astype(jnp.float32)
            out[pos_ref[base + c]] = step.astype(out.dtype)

    @pl.when(s == 0)
    def _():
        run(gu, wu)

    @pl.when(s == 1)
    def _():
        run(gd, wd)


def packed_steps(pos, gu, gd, wu, wd, moment_one, moment_two):
    owned, rows, width = gu.shape
    cols = width // 128
    moment = pl.BlockSpec((1, 1, 1, rows, width), lambda s, i, p: (s, 0, i, 0, 0))
    first = pl.BlockSpec((1, rows, width), lambda s, i, p: (i * (1 - s) + (owned - 1) * s, 0, 0))
    second = pl.BlockSpec((1, rows, width), lambda s, i, p: (i * s, 0, 0))
    tiles = 2 * owned * cols
    return pl.pallas_call(
        functools.partial(step_kernel, cols, owned),
        out_shape=jax.ShapeDtypeStruct((tiles, rows, 128), jnp.bfloat16),
        grid_spec=pltpu.PrefetchScalarGridSpec(
            num_scalar_prefetch=1,
            grid=(2, owned),
            in_specs=[first, second, first, second, moment, moment],
            out_specs=pl.BlockSpec((tiles, rows, 128), lambda s, i, p: (0, 0, 0)),
        ),
        compiler_params=pltpu.CompilerParams(vmem_limit_bytes=40 * 2**20),
        name="packed_steps",
    )(pos, gu, gd, wu, wd, moment_one, moment_two)


def spread_kernel(cols, per, table, packed, out):
    base = pl.program_id(0) * per * cols

    def bucket(k, carry):
        for c in range(cols):
            index = table[base + k * cols + c]
            at = slice(c * 128, (c + 1) * 128)

            @pl.when(index >= 0)
            def _():
                out[k, :, at] = packed[jnp.maximum(index, 0)]

            @pl.when(index < 0)
            def _():
                out[k, :, at] = jnp.zeros((out.shape[1], 128), out.dtype)

        return carry

    lax.fori_loop(0, per, bucket, 0)


def spread_steps(table, packed, total, cols):
    rows = packed.shape[1]
    per = 4
    return pl.pallas_call(
        functools.partial(spread_kernel, cols, per),
        out_shape=jax.ShapeDtypeStruct((total, rows, cols * 128), packed.dtype),
        grid_spec=pltpu.PrefetchScalarGridSpec(
            num_scalar_prefetch=1,
            grid=(total // per,),
            in_specs=[pl.BlockSpec(memory_space=pltpu.VMEM)],
            out_specs=pl.BlockSpec((per, rows, cols * 128), lambda i, t: (i, 0, 0)),
        ),
        compiler_params=pltpu.CompilerParams(vmem_limit_bytes=48 * 2**20),
        name="spread_steps",
    )(table, packed)


def shards(
    n_dp,
    n_mp,
    tokens_in,
    out_grad,
    w_up,
    w_down,
    mask_up,
    mask_down,
    order_up,
    order_down,
    moment_one,
    moment_two,
):
    hidden_local, width = w_up.shape
    buckets = order_up.shape[0]
    owned = buckets // n_dp
    bucket_rows = hidden_local // buckets
    cols = width // 128
    tiles = 2 * owned * cols
    owner_index = lax.axis_index("dp")
    row_of = jnp.arange(buckets) * bucket_rows // 128

    def by_owner(order):
        where = jnp.zeros((buckets,), jnp.int32).at[order].set(jnp.arange(buckets, dtype=jnp.int32))
        return where.reshape(owned, n_dp).T

    slots_up, slots_down = by_owner(order_up), by_owner(order_down)
    live = jnp.concatenate([mask_up[row_of[slots_up]], mask_down[row_of[slots_down]]], axis=1)
    live = live.reshape(n_dp, tiles)
    ahead = jnp.cumsum(live, axis=1)
    count = ahead[:, -1:]
    index = jnp.arange(tiles, dtype=jnp.int32)[None]
    pos = jnp.where(live > 0, ahead - 1, count + index - ahead).astype(jnp.int32)
    most = lax.pmax(jnp.max(count).astype(jnp.float32), "mp")
    pos_cube = pos.reshape(n_dp, 2, owned, cols)

    def live_part(weight, mask):
        blocks = weight.reshape(hidden_local // 128, 128, cols, 128)
        return (blocks * mask.astype(weight.dtype)[:, None, :, None]).reshape(hidden_local, width)

    up_live = live_part(w_up, mask_up)
    down_live = live_part(w_down, mask_down)
    mine_up, mine_down = slots_up[owner_index], slots_down[owner_index]

    def mm(a, b, dims):
        return lax.dot_general(a, b, (dims, ((), ())), preferred_element_type=jnp.float32)

    def rows_of(matrix, chosen):
        return matrix.reshape(buckets, bucket_rows, width)[chosen]

    gathered = n_dp * n_mp <= 64
    if gathered:
        x_all, g_all = gather_all(tokens_in, out_grad, n_dp, n_mp)
        group = x_all.shape[0] // n_dp
        x_rep = lax.dynamic_slice_in_dim(x_all, owner_index * group, group, 0)
        g_rep = lax.dynamic_slice_in_dim(g_all, owner_index * group, group, 0)
    else:
        x_rep = lax.all_gather(tokens_in, "mp", axis=0, tiled=True)
        g_rep = lax.all_gather(out_grad, "mp", axis=0, tiled=True)

    activation, gelu_back = jax.vjp(jax.nn.gelu, mm(x_rep, up_live, ((1,), (1,))))
    hidden_grad = gelu_back(mm(g_rep, down_live, ((1,), (1,))))[0].astype(jnp.bfloat16)
    partial_term = mm(hidden_grad, up_live, ((1,), (0,))).astype(jnp.bfloat16)
    if gathered:
        partial_term, x_all, g_all = lax.optimization_barrier((partial_term, x_all, g_all))
    input_grad = lax.psum_scatter(partial_term, "mp", scatter_dimension=0, tiled=True)

    if gathered:
        up_rows = rows_of(up_live, jnp.concatenate([mine_up, mine_down])).reshape(-1, width)
        down_rows = rows_of(down_live, mine_up).reshape(-1, width)
        half = owned * bucket_rows
        pre = mm(x_all, up_rows, ((1,), (1,)))
        act_low = jax.nn.gelu(pre[:, half:]).astype(jnp.bfloat16)
        _, owner_back = jax.vjp(jax.nn.gelu, pre[:, :half])
        grad_low = owner_back(mm(g_all, down_rows, ((1,), (1,))))[0].astype(jnp.bfloat16)
        grad_up = mm(grad_low, x_all, ((0,), (0,)))
        grad_down = mm(act_low, g_all, ((0,), (0,)))
    else:

        def to_owner(part, slots):
            by_slot = rows_of(part.astype(jnp.bfloat16), slots.reshape(-1))
            return lax.psum_scatter(by_slot, "dp", scatter_dimension=0, tiled=True)

        act_low = activation.astype(jnp.bfloat16)
        grad_up = to_owner(mm(hidden_grad, x_rep, ((0,), (0,))), slots_up).astype(jnp.float32)
        grad_down = to_owner(mm(act_low, g_rep, ((0,), (0,))), slots_down).astype(jnp.float32)
    packed = packed_steps(
        pos[owner_index],
        grad_up.reshape(owned, bucket_rows, width),
        grad_down.reshape(owned, bucket_rows, width),
        rows_of(w_up, mine_up),
        rows_of(w_down, mine_down),
        moment_one,
        moment_two,
    )

    def table_for(order, mask, matrix, size):
        owner, slot = order % n_dp, order // n_dp
        found = owner[:, None] * size + pos_cube[owner, matrix, slot]
        return jnp.where(mask[row_of] > 0, found, -1)

    def send(size, packed):
        table = jnp.concatenate(
            [table_for(order_up, mask_up, 0, size), table_for(order_down, mask_down, 1, size)]
        ).astype(jnp.int32)
        arrived = lax.all_gather(packed[:size], "dp", axis=0, tiled=True)
        return spread_steps(table.reshape(-1), arrived, 2 * buckets, cols)

    sizes = [-(-tiles * part // 12) for part in (6, 7, 8, 10, 12)]
    level = jnp.sum(most > jnp.asarray(sizes[:-1], jnp.float32)).astype(jnp.int32)
    steps = lax.switch(level, [functools.partial(send, size) for size in sizes], packed)
    return (input_grad, steps.reshape(2, hidden_local, width))


def solution(mesh):
    placed = (
        P(("dp", "mp"), None),
        P(("dp", "mp"), None),
        P("mp", None),
        P("mp", None),
        P("mp", None),
        P("mp", None),
        P(),
        P(),
        P(None, "mp", "dp", None, None),
        P(None, "mp", "dp", None, None),
    )
    return jax.shard_map(
        functools.partial(shards, mesh.shape["dp"], mesh.shape["mp"]),
        mesh=mesh,
        in_specs=placed,
        out_specs=(P(("dp", "mp"), None), P(None, "mp", None)),
        check_vma=False,
    )
```

time: 840 us -> 625 us (0.74); the launches traced: 839 us -> 616 us
  waiting for transfers between devices: 627 us -> 246 us
  Pallas kernels: 0 us -> 176 us
  local copies, waits for them, and re-layouts: 102 us -> 54.3 us
  matrix products: 56.8 us -> 86.8 us
  other arithmetic: 38.6 us -> 23 us
  blocking collectives: 0 us -> 12.9 us
    reduce_scatter x3 -> x1, waiting for transfers between devices: 268 us -> 48.4 us  [shards(): lax.psum_scatter(partial_term, 'mp', scatter_dimension=0, tiled=True)]
    pallas_call x0 -> x3, Pallas kernels: none -> 176 us  [the longest x1 115 us: gather_all(): pl.pallas_call(functools.partial(gather_kernel, n_dp, n_mp), out_shape=(s...]
    all_gather x3 -> x1, waiting for transfers between devices: 358 us -> 197 us  [send(): arrived = lax.all_gather(packed[:size], 'dp', axis=0, tiled=True)]
    gather x8 -> x16, local copies, waits for them, and re-layouts: 62.6 us -> 29.1 us  [the longest x4 22.9 us: rows_of(): return matrix.reshape(buckets, bucket_rows, width)[chosen]]
    another operation x3 -> x2, other arithmetic: 32.3 us -> 1.33 us  [the longest x1 16.5 us: shards(): return (input_grad, jnp.stack([update_up, update_down]))]
    dot_general x5, matrix products: 56.8 us -> 86.8 us  [mm(): lax.dot_general(a, b, (dims, ((), ())), preferred_element_type=jnp.float32)]
    broadcast_in_dim x6 -> x2, local copies, waits for them, and re-layouts: 16.8 us -> 0.17 us  [the longest x1 0.09 us: shards(): row_of[slots_up]]
    mul x0 -> x3, other arithmetic: none -> 16.1 us  [the longest x2 16.1 us: live_part(): blocks * mask.astype(weight.dtype)[:, None, :, None]]
  transfers between devices with their start and end apart: 6 -> 2, of which waited for: 5 -> 2; matrix products, arithmetic and copies ran while one was open for 16% -> 1% of each run, Pallas kernels for 0% -> 0%
where the time goes in v1:
time: 625 us; the launch traced here: 616 us
  waiting for transfers between devices  246 us (39%)
  Pallas kernels  176 us (28%)
  matrix products  86.8 us (14%)
  local copies, waits for them, and re-layouts  54.3 us (9%)
  other arithmetic  23 us (4%)
  between operations  17.2 us (3%)
  blocking collectives  12.9 us (2%)
    all_gather x1, waiting for transfers between devices, send(): arrived = lax.all_gather(packed[:size], 'dp', axis=0, tiled=True)  197 us
    pallas_call x1, Pallas kernels, gather_all(): pl.pallas_call(functools.partial(gather_kernel, n_dp, n_mp), out_shape=(s...  115 us
    dot_general x5, matrix products, mm(): lax.dot_general(a, b, (dims, ((), ())), preferred_element_type=jnp.float32)  86.8 us
    reduce_scatter x1, waiting for transfers between devices, shards(): lax.psum_scatter(partial_term, 'mp', scatter_dimension=0, tiled=True)  48.4 us
    pallas_call x1, Pallas kernels, spread_steps(): pl.pallas_call(functools.partial(spread_kernel, cols, per), out_shape=jax...  39.2 us
    gather x4, local copies, waits for them, and re-layouts, rows_of(): return matrix.reshape(buckets, bucket_rows, width)[chosen]  22.9 us
    pallas_call x1, Pallas kernels, packed_steps(): pl.pallas_call(functools.partial(step_kernel, cols, owned), out_shape=jax...  21.2 us
    mul x2, other arithmetic, live_part(): blocks * mask.astype(weight.dtype)[:, None, :, None]  16.1 us
  transfers between devices with their start and end apart: 2, of which 2 were waited for; matrix products, arithmetic and copies ran while one was open for 1% of the time, Pallas kernels for 0%

profile of v1, /device:TPU:0, one launch (start us, length us, event | category | flops | bytes accessed | tf_op | source)
XLA Modules:
  0.0 615.7 jit_solution(8228136928130188416)
XLA Ops:
  8.0 0.7 convert_element_type.25
  12.8 0.8 gather_fusion.20
  13.9 0.8 gather_fusion.22
  16.3 1.1 reduce-window.6
  18.8 115.1 %gather_tokens.1 = (bf16[32,64,3072]{2,1,0:T(8,128)(2,1)}, bf16[32,64,3072]{2,1,0:T(8,128)(2,1)}) custom-call(bf16[64,3072]{1,0:T(8,128)(2,1)} %x_ref.1, bf16[64,3072]{1,0:T(8,128)(2,1)} %g_ref.1), custom_call_target="tpu_custom_call" | custom-call | tf_op jit(solution)/shard_map/gather_tokens/pallas_call | solution.py:126
  133.9 6.1 mul.210
  140.0 1.0 copy-done.5
  141.0 10.0 %fusion.79 = f32[512,1536]{1,0:T(8,128)} fusion(bf16[2048,3072]{1,0:T(8,128)(2,1)} %bitcast.83, s32[]{:T(128)S(6)} %select_n.285, bf16[1536,3072]{1,0:T(8,128)(2,1)S(1)} %copy-done.5, bf16[192,8,24,128]{3,2,1,0:T(8,128)(2,1)} %bitcast.71), kind=kOutput, calls=%fused_computation.234 | convolution fusion | flops 4836556800 | bytes 25165828 | tf_op jit(solution)/shard_map/dot_general | solution.py:274
  151.0 4.9 mul.207
  155.8 23.6 %convolution_convert_fusion = bf16[512,3072]{1,0:T(8,128)(2,1)} fusion(bf16[1536,3072]{1,0:T(8,128)(2,1)} %param.18, bf16[192,8,24,128]{3,2,1,0:T(8,128)(2,1)} %bitcast.72, f32[512,1536]{1,0:T(8,128)} %fusion.79, bf16[1536,3072]{1,0:T(8,128)(2,1)} %param.19, bf16[192,8,24,128]{3,2,1,0:T(8,128)(2,1)} %bitcast.73, bf16[2048,3072]{1,0:T(8,128)(2,1)} %bitcast.86, ...), kind=kOutput, calls=%fused_computation.211 | convolution fusion | flops 9690415104 | bytes 47185924 | tf_op jit(solution)/shard_map/dot_general | solution.py:274
  180.0 8.1 %broadcast_multiply_fusion.10 = bf16[48,32,3072]{2,1,0:T(8,128)(2,1)} fusion(bf16[48,32,3072]{2,1,0:T(8,128)(2,1)} %bitcast.67, bf16[48,3072]{1,0:T(8,128)(2,1)S(1)} %bitcast.78), kind=kLoop, calls=%fused_computation.205 | loop fusion | flops 4718592 | bytes 19169280 | tf_op jit(solution)/shard_map/mul | solution.py:267
  188.2 4.4 gather_fusion.26
  192.5 8.0 %broadcast_multiply_fusion.11 = bf16[48,32,3072]{2,1,0:T(8,128)(2,1)} fusion(bf16[48,32,3072]{2,1,0:T(8,128)(2,1)} %bitcast.69, bf16[48,3072]{1,0:T(8,128)(2,1)S(1)} %bitcast.79), kind=kLoop, calls=%fused_computation.206 | loop fusion | flops 4718592 | bytes 19169280 | tf_op jit(solution)/shard_map/mul | solution.py:267
  200.5 5.8 gather_fusion.24
  206.4 6.9 %gather_fusion.25 = bf16[24,32,3072]{2,1,0:T(8,128)(2,1)} fusion(bf16[48,32,3072]{2,1,0:T(8,128)(2,1)} %broadcast_multiply_fusion.10, s32[1024]{0:T(1024)S(1)} %pad_clamp_fusion.11), kind=kCustom, calls=%fused_computation.25 | custom fusion | bytes 9437280 | tf_op jit(solution)/shard_map/gather | solution.py:277
  213.2 14.3 %fusion.126 = f32[2048,768]{1,0:T(8,128)S(1)} fusion(bf16[2048,3072]{1,0:T(8,128)(2,1)} %bitcast.84, bf16[768,3072]{1,0:T(8,128)(2,1)} %bitcast.74), kind=kOutput, calls=%fused_computation.309 | convolution fusion | flops 9663676416 | bytes 23592960 | tf_op jit(solution)/shard_map/dot_general | solution.py:274
  227.6 13.4 %fusion.84 = f32[384,3072]{1,0:T(8,128)} fusion(bf16[2048,3072]{1,0:T(8,128)(2,1)} %bitcast.87, f32[2048,768]{1,0:T(8,128)S(1)} %fusion.126), kind=kOutput, calls=%fused_computation.238 | convolution fusion | flops 4838916096 | bytes 20447232 | tf_op jit(solution)/shard_map/dot_general | solution.py:274
  241.0 25.4 %fusion.82 = f32[384,3072]{1,0:T(8,128)} fusion(bf16[2048,3072]{1,0:T(8,128)(2,1)} %bitcast.85, f32[2048,768]{1,0:T(8,128)} %copy-done.9, bf16[2048,3072]{1,0:T(8,128)(2,1)} %bitcast.88, bf16[384,3072]{1,0:T(8,128)(2,1)} %bitcast.75), kind=kOutput, calls=%fused_computation.237 | convolution fusion | flops 9679405056 | bytes 35389440 | tf_op jit(solution)/shard_map/dot_general | solution.py:274
  267.1 5.9 gather_fusion.27
  273.0 12.9 %pmax.7 = f32[]{:T(128)} all-reduce(f32[]{:T(128)S(6)} %convert_element_type.28), channel_id=1, replica_groups=mesh['dp'=4,'mp'=8] {'mp'}, use_global_device_ids=true, to_apply=%region_6.7 | all-reduce | flops 1 | bytes 8 | tf_op jit(solution)/shard_map/pmax | solution.py:262
  285.9 1.3 fusion.102
  287.9 1.7 copy-done
  289.5 2.3 copy-done.1
  291.9 2.3 copy-done.2
  294.2 21.2 %packed_steps.1 = bf16[576,32,128]{2,1,0:T(8,128)(2,1)} custom-call(s32[576]{0:T(1024)S(1)} %dynamic-slice_reduce_fusion.pos_ref, f32[12,32,3072]{2,1,0:T(8,128)S(1)} %bitcast.61, f32[12,32,3072]{2,1,0:T(8,128)S(1)} %bitcast.60, bf16[12,32,3072]{2,1,0:T(8,128)(2,1)S(1)} %gather_fusion.26, bf16[12,32,3072]{2,1,0:T(8,128)(2,1)S(1)} %copy-done, ...), custom_call_target="tpu_custom_call" | custom-call | tf_op jit(solution)/shard_map/packed_steps/pallas_call | solution.py:176
  315.4 243.7 %conditional.1 = (bf16[2,1536,3072]{2,1,0:T(8,128)(2,1)}) conditional(s32[]{:T(128)} %clamp.3, (s32[48]{0:T(128)S(1)}, s32[48]{0:T(128)S(1)}, s32[12,24]{1,0:T(8,128)S(1)}, s32[48]{0:T(128)S(1)}, s32[4,2,12,24]{3,2,1,0:T(8,128)S(1)}, /*index=5*/s32[12,24]{1,0:T(8,128)S(1)}, s32[48]{0:T(128)S(1)}, ...), branch_computations={%region_8.9_spmd, %region_9.10_spmd, %region_10.11_spmd, %region_1... | conditional | flops 14576 | bytes 70911152 | solution.py:339
  315.5 3.8 slice.22
  319.3 1.0 gather_fusion.5
  320.4 1.0 gather_fusion.7
  322.8 197.0 %all-gather.8.cloned.1.call-done.packed = bf16[1344,32,128]{2,1,0:T(8,128)(2,1)} async-done(((bf16[336,32,128]{2,1,0:T(8,128)(2,1)}), bf16[1344,32,128]{2,1,0:T(8,128)(2,1)}) %all-gather.8.cloned.1.call-update) | async-done | bytes 11010064 | tf_op jit(solution)/shard_map/cond/branch_1_fun/all_gather | solution.py:334
  519.8 39.2 %spread_steps.6 = bf16[96,32,3072]{2,1,0:T(8,128)(2,1)} custom-call(s32[2304]{0:T(1024)S(1)} %reshape.192.table, bf16[1344,32,128]{2,1,0:T(8,128)(2,1)} %all-gather.8.cloned.1.call-done.packed), custom_call_target="tpu_custom_call" | custom-call | tf_op jit(solution)/shard_map/cond/branch_1_fun/spread_steps/pallas_call | solution.py:214
  559.6 48.4 %reduce-scatter.2.cloned.1.call-done = bf16[64,3072]{1,0:T(8,128)(2,1)} async-done(((bf16[512,3072]{1,0:T(8,128)(2,1)}), bf16[64,3072]{1,0:T(8,128)(2,1)}) %reduce-scatter.2.cloned.1.call-update) | async-done | bytes 393232 | tf_op jit(solution)/shard_map/reduce_scatter | solution.py:294
  (83 shorter events, 9.9 us)
Async XLA Ops:
  8.0 6.8 %copy-start.3 = (s32[12,24]{1,0:T(8,128)S(1)}, s32[12,24]{1,0:T(8,128)}, u32[]{:S(2)}) copy-start(s32[12,24]{1,0:T(8,128)} %param.20) | copy-start | bytes 3460
  8.0 7.5 %copy-start.4 = (s32[12,24]{1,0:T(8,128)S(1)}, s32[12,24]{1,0:T(8,128)}, u32[]{:S(2)}) copy-start(s32[12,24]{1,0:T(8,128)} %param.21) | copy-start | bytes 3460
  133.9 7.1 %copy-start.5 = (bf16[1536,3072]{1,0:T(8,128)(2,1)S(1)}, bf16[1536,3072]{1,0:T(8,128)(2,1)}, u32[]{:S(2)}) copy-start(bf16[1536,3072]{1,0:T(8,128)(2,1)} %param.18) | copy-start | bytes 28311556
  227.5 13.5 %copy-start.9 = (f32[2048,768]{1,0:T(8,128)}, f32[2048,768]{1,0:T(8,128)S(1)}, u32[]{:S(2)}) copy-start(f32[2048,768]{1,0:T(8,128)S(1)} %fusion.126) | copy-start | bytes 18874372
  266.5 19.4 %copy-start.8 = (f32[4]{0:T(128)S(1)}, f32[4]{0:T(128)}, u32[]{:S(2)}) copy-start(f32[4]{0:T(128)} %constant.297.clone) | copy-start | bytes 52
  287.9 1.7 copy-start
  289.5 2.3 copy-start.1
  291.9 2.3 copy-start.2
  294.2 21.2 %copy-start.6 = (s32[48]{0:T(128)S(1)}, s32[48]{0:T(128)}, u32[]{:S(2)}) copy-start(s32[48]{0:T(128)} %param.23) | copy-start | bytes 580
  294.2 21.2 %copy-start.7 = (s32[48]{0:T(128)S(1)}, s32[48]{0:T(128)}, u32[]{:S(2)}) copy-start(s32[48]{0:T(128)} %param.22) | copy-start | bytes 580
  315.4 204.4 %all-gather.8.cloned.1.call-start = ((), (), s32[]{:S(2)}) async-start(), calls=%async_computation.2 | async-start | bytes 13762560 | tf_op jit(solution)/shard_map/cond/branch_1_fun/all_gather | solution.py:334
  559.1 49.0 %reduce-scatter.2.cloned.1.call-start = ((), (), s32[]{:S(2)}) async-start(), calls=%async_computation.6 | async-start | bytes 3538944 | tf_op jit(solution)/shard_map/reduce_scatter | solution.py:294
Sparse Core Ops, SparseCore 0:
  319.4 200.4 all-gather.7
Sparse Core Ops, SparseCore 1:
  563.5 44.5 reduce-scatter.1
